TPU v7x, 32 devices: a whole 2x2x4 slice. The times are simulated.
32 devices in a mesh: row: 8 (over z, x), col: 4 (over y, core).
Axes of the slice: x: 2, y: 2, z: 4, core: 2. Of those that a mesh axis runs over, the one named last changes fastest.
Arguments:
- right_sides: bfloat16 [4, 32, 256, 256], P(None, ('row', 'col')), may hold values from -6 to 6
- lower_blocks: bfloat16 [8, 4, 3, 6, 256, 256], P('row', 'col'), may hold values from -0.1875 to 0.1875
- lower_source: int32 [8, 4, 3, 6], P('row', 'col'), may hold values from 0 to 7
- lower_target: int32 [8, 4, 3, 6], P('row', 'col'), may hold values from 4 to 16, as said below
- diag_lower_inv: bfloat16 [4, 32, 256, 256], P(None, ('row', 'col')), may hold values from -1 to 2, as said below
- upper_blocks: bfloat16 [8, 4, 3, 6, 256, 256], P('row', 'col'), may hold values from -0.1875 to 0.1875
- upper_source: int32 [8, 4, 3, 6], P('row', 'col'), may hold values from 0 to 7
- upper_target: int32 [8, 4, 3, 6], P('row', 'col'), may hold values from 0 to 16, as said below
- diag_upper_inv: bfloat16 [4, 32, 256, 256], P(None, ('row', 'col')), may hold values from -1 to 2, as said below
Outputs:
- solution: float32 [4, 32, 256, 256], P(None, ('row', 'col'))
Inputs may be any that keep to these rules, and one draw needn't show every extreme that they name: lower_target[r, c, a, k] is 16 for an empty slot, else b * 4 + q with a < b < 4 and 0 <= q < 4. upper_target[r, c, a, k] is 16 for an empty slot, else b * 4 + q with 0 <= b <= a and 0 <= q < 4. `diag_lower_inv`: each block is lower triangular with a positive diagonal. `diag_upper_inv`: each block is upper triangular with a positive diagonal.
All inputs are finite; a program needn't handle non-finite values.
Results may differ from a plain program's by a relative error of at most 0.029.
Values may be sent and summed in bfloat16 or wider, within the bound.
A program may use at most 128 MiB of HBM per device.

v0:
```python
import jax
import jax.numpy as jnp
from jax import lax
from jax.sharding import PartitionSpec as P


def fetch_sources(solved_panel, source_ids):
    gathered = lax.all_gather(solved_panel, "row", axis=0, tiled=True)
    return jnp.take(gathered, source_ids, axis=0)


def block_updates(chosen, blocks, target_ids, first_row, row_count):
    products = jnp.einsum("kij,kjm->kim", blocks, chosen, preferred_element_type=jnp.float32)
    rows_wanted = jnp.arange(row_count, dtype=jnp.int32) + first_row
    selector = (rows_wanted[:, None] == target_ids[None, :]).astype(jnp.float32)
    return jnp.einsum("qk,kim->qim", selector, products, precision=lax.Precision.HIGHEST)


def row_share(partial_level):
    return lax.psum_scatter(
        partial_level.astype(jnp.bfloat16), "col", scatter_dimension=0, tiled=True
    ).astype(jnp.float32)


def diag_apply(inverse, vector):
    return jnp.einsum(
        "sij,sjm->sim", inverse, vector.astype(jnp.bfloat16), preferred_element_type=jnp.float32
    )


def solve_columns(
    right_sides,
    lower_blocks,
    lower_source,
    lower_target,
    diag_lower_inv,
    upper_blocks,
    upper_source,
    upper_target,
    diag_upper_inv,
):
    levels = right_sides.shape[0]
    per_device = right_sides.shape[1]
    block_width = right_sides.shape[2]
    rhs_cols = right_sides.shape[3]
    local_rows = lax.axis_size("col") * per_device
    buffer_shape = (levels, local_rows, block_width, rhs_cols)
    partial_value = jnp.zeros(buffer_shape, jnp.float32)
    forward = []
    for tree_level in range(levels):
        lowered = right_sides[tree_level].astype(jnp.float32)
        if tree_level > 0:
            lowered = lowered - row_share(partial_value[tree_level])
        result = diag_apply(diag_lower_inv[tree_level], lowered)
        forward.append(result)
        if tree_level + 1 < levels:
            chosen = fetch_sources(result.astype(jnp.bfloat16), lower_source[0, 0, tree_level])
            levels_above = levels - tree_level - 1
            updates = block_updates(
                chosen,
                lower_blocks[0, 0, tree_level],
                lower_target[0, 0, tree_level],
                (tree_level + 1) * local_rows,
                levels_above * local_rows,
            )
            partial_value = partial_value.at[tree_level + 1 :].add(
                updates.reshape((levels_above, local_rows, block_width, rhs_cols))
            )
    partial_value = jnp.zeros(buffer_shape, jnp.float32)
    solution = [None] * levels
    for tree_level in range(levels - 1, -1, -1):
        raised = forward[tree_level]
        if tree_level + 1 < levels:
            raised = raised - row_share(partial_value[tree_level])
        result = diag_apply(diag_upper_inv[tree_level], raised)
        solution[tree_level] = result
        if tree_level > 0:
            chosen = fetch_sources(result.astype(jnp.bfloat16), upper_source[0, 0, tree_level - 1])
            updates = block_updates(
                chosen,
                upper_blocks[0, 0, tree_level - 1],
                upper_target[0, 0, tree_level - 1],
                0,
                tree_level * local_rows,
            )
            partial_value = partial_value.at[:tree_level].add(
                updates.reshape((tree_level, local_rows, block_width, rhs_cols))
            )
    return jnp.stack(solution)


def shards(
    right_sides,
    lower_blocks,
    lower_source,
    lower_target,
    diag_lower_inv,
    upper_blocks,
    upper_source,
    upper_target,
    diag_upper_inv,
):
    return solve_columns(
        right_sides,
        lower_blocks,
        lower_source,
        lower_target,
        diag_lower_inv,
        upper_blocks,
        upper_source,
        upper_target,
        diag_upper_inv,
    )


def solution(mesh):
    in_specs = (
        P(None, ("row", "col"), None, None),
        P("row", "col", None, None, None, None),
        P("row", "col", None, None),
        P("row", "col", None, None),
        P(None, ("row", "col"), None, None),
        P("row", "col", None, None, None, None),
        P("row", "col", None, None),
        P("row", "col", None, None),
        P(None, ("row", "col"), None, None),
    )
    out_specs = P(None, ("row", "col"), None, None)
    return jax.shard_map(shards, mesh=mesh, in_specs=in_specs, out_specs=out_specs, check_vma=False)
```

profile of v0, /device:TPU:1, one launch (start us, length us, event | category | flops | bytes accessed | tf_op | source)
XLA Modules:
  0.0 464.1 jit_solution(1144032115119934765)
XLA Ops:
  6.5 1.9 fusion.116
  8.5 0.7 compare_and_fusion.3
  9.2 0.7 slice_bitcast_fusion.2
  9.9 40.8 %all-gather.13.cloned.1.call-done = bf16[2048,256]{1,0:T(8,128)(2,1)} async-done(((bf16[256,256]{1,0:T(8,128)(2,1)}), bf16[2048,256]{1,0:T(8,128)(2,1)}) %all-gather.13.cloned.1.call-update) | async-done | bytes 1048592 | tf_op jit(solution)/shard_map/all_gather | solution.py:8
  50.8 1.8 gather_fusion
  52.6 2.8 convolution_bitcast_fusion.5
  55.4 2.1 copy.56
  57.5 2.1 fusion.92
  59.7 2.0 copy-done.1
  61.6 0.3 slice.446
  61.9 0.9 copy.57
  62.8 21.5 %reduce-scatter.7.cloned.1.call-done = bf16[1,256,256]{2,1,0:T(8,128)(2,1)} async-done(((bf16[4,256,256]{2,1,0:T(8,128)(2,1)}), bf16[1,256,256]{2,1,0:T(8,128)(2,1)}) %reduce-scatter.7.cloned.1.call-update) | async-done | bytes 131088 | tf_op jit(solution)/shard_map/reduce_scatter | solution.py:20
  84.4 1.8 bitcast_convert_fusion.4
  86.3 39.6 %all-gather.15.cloned.1.call-done = bf16[2048,256]{1,0:T(8,128)(2,1)} async-done(((bf16[256,256]{1,0:T(8,128)(2,1)}), bf16[2048,256]{1,0:T(8,128)(2,1)}) %all-gather.15.cloned.1.call-update) | async-done | bytes 1048592 | tf_op jit(solution)/shard_map/all_gather | solution.py:8
  125.9 1.8 gather_fusion.1
  127.7 1.6 convolution_bitcast_fusion.4
  129.4 1.9 copy.60
  131.3 4.1 slice_add_fusion
  135.6 0.9 copy.61
  136.5 21.5 %reduce-scatter.9.cloned.1.call-done = bf16[1,256,256]{2,1,0:T(8,128)(2,1)} async-done(((bf16[4,256,256]{2,1,0:T(8,128)(2,1)}), bf16[1,256,256]{2,1,0:T(8,128)(2,1)}) %reduce-scatter.9.cloned.1.call-update) | async-done | bytes 131088 | tf_op jit(solution)/shard_map/reduce_scatter | solution.py:20
  158.0 1.9 bitcast_convert_fusion.3
  160.1 37.2 %all-gather.17.cloned.1.call-done = bf16[2048,256]{0,1:T(8,128)(2,1)} async-done(((bf16[256,256]{0,1:T(8,128)(2,1)}), bf16[2048,256]{0,1:T(8,128)(2,1)}) %all-gather.17.cloned.1.call-update) | async-done | bytes 1048592 | tf_op jit(solution)/shard_map/all_gather | solution.py:8
  197.2 1.5 copy.87
  198.7 1.5 gather_fusion.2
  200.2 3.0 convolution_bitcast_fusion.3
  203.2 2.9 copy.64
  206.1 2.9 fusion
  209.1 0.9 copy.65
  210.0 23.1 %reduce-scatter.11.cloned.1.call-done = bf16[1,256,256]{2,1,0:T(8,128)(2,1)} async-done(((bf16[4,256,256]{2,1,0:T(8,128)(2,1)}), bf16[1,256,256]{2,1,0:T(8,128)(2,1)}) %reduce-scatter.11.cloned.1.call-update) | async-done | bytes 131088 | tf_op jit(solution)/shard_map/reduce_scatter | solution.py:20
  233.1 2.1 bitcast_convert_fusion.2
  235.5 37.0 %all-gather.19.cloned.1.call-done = bf16[2048,256]{0,1:T(8,128)(2,1)} async-done(((bf16[256,256]{0,1:T(8,128)(2,1)}), bf16[2048,256]{0,1:T(8,128)(2,1)}) %all-gather.19.cloned.1.call-update) | async-done | bytes 1048592 | tf_op jit(solution)/shard_map/all_gather | solution.py:8
  272.5 1.5 copy.88
  274.0 0.6 gather_fusion.3
  274.6 2.8 convolution_bitcast_fusion.2
  277.4 2.1 copy.68
  279.5 2.1 fusion.86
  281.7 2.0 copy-done
  283.7 0.3 slice.347
  283.9 1.1 copy.92
  285.1 23.1 %reduce-scatter.13.cloned.1.call-done = bf16[1,256,256]{1,2,0:T(8,128)(2,1)} async-done(((bf16[4,256,256]{1,2,0:T(8,128)(2,1)}), bf16[1,256,256]{1,2,0:T(8,128)(2,1)}) %reduce-scatter.13.cloned.1.call-update) | async-done | bytes 131088 | tf_op jit(solution)/shard_map/reduce_scatter | solution.py:20
  308.2 1.8 bitcast_convert_fusion.1
  310.1 37.3 %all-gather.21.cloned.1.call-done = bf16[2048,256]{0,1:T(8,128)(2,1)} async-done(((bf16[256,256]{0,1:T(8,128)(2,1)}), bf16[2048,256]{0,1:T(8,128)(2,1)}) %all-gather.21.cloned.1.call-update) | async-done | bytes 1048592 | tf_op jit(solution)/shard_map/all_gather | solution.py:8
  347.4 1.5 copy.89
  348.8 0.6 gather_fusion.4
  349.5 2.8 convolution_bitcast_fusion.1
  352.3 2.1 copy.73
  354.4 1.1 fusion.89
  355.5 0.5 slice-done
  356.0 1.2 copy_add_fusion
  357.2 1.3 copy-done.2
  358.5 0.8 slice.444
  359.4 23.1 %reduce-scatter.15.cloned.1.call-done = bf16[1,256,256]{2,1,0:T(8,128)(2,1)} async-done(((bf16[4,256,256]{2,1,0:T(8,128)(2,1)}), bf16[1,256,256]{2,1,0:T(8,128)(2,1)}) %reduce-scatter.15.cloned.1.call-update) | async-done | bytes 131088 | tf_op jit(solution)/shard_map/reduce_scatter | solution.py:20
  382.5 1.9 bitcast_convert_fusion
  384.5 37.5 %all-gather.23.cloned.1.call-done = bf16[2048,256]{0,1:T(8,128)(2,1)} async-done(((bf16[256,256]{0,1:T(8,128)(2,1)}), bf16[2048,256]{0,1:T(8,128)(2,1)}) %all-gather.23.cloned.1.call-update) | async-done | bytes 1048592 | tf_op jit(solution)/shard_map/all_gather | solution.py:8
  421.9 1.5 copy.90
  423.4 0.6 gather_fusion.5
  424.0 2.8 convolution_bitcast_fusion
  426.8 2.1 copy.77
  428.9 1.1 fusion.103
  430.0 0.5 copy-done.3
  430.5 1.0 fusion.2
  431.5 23.1 %reduce-scatter.17.cloned.1.call-done = bf16[1,256,256]{2,1,0:T(8,128)(2,1)} async-done(((bf16[4,256,256]{2,1,0:T(8,128)(2,1)}), bf16[1,256,256]{2,1,0:T(8,128)(2,1)}) %reduce-scatter.17.cloned.1.call-update) | async-done | bytes 131088 | tf_op jit(solution)/shard_map/reduce_scatter | solution.py:20
  454.6 1.2 convolution_bitcast_fusion.6
  455.9 1.3 copy.79
  (54 shorter events, 1.2 us)
Async XLA Ops:
  6.5 44.2 %all-gather.13.cloned.1.call-start = ((), (), s32[]{:S(2)}) async-start(), calls=%async_computation.12 | async-start | bytes 1179648 | tf_op jit(solution)/shard_map/all_gather | solution.py:8
  8.5 75.9 %reduce-scatter.7.cloned.1.call-start = ((), (), s32[]{:S(2)}) async-start(), calls=%async_computation.6 | async-start | bytes 655360 | tf_op jit(solution)/shard_map/reduce_scatter | solution.py:20
  59.6 2.0 copy-start.1
  61.6 22.7 %copy-start.7 = (bf16[4,1,256,256]{3,2,1,0:T(8,128)(2,1)S(1)}, bf16[4,1,256,256]{3,2,1,0:T(8,128)(2,1)}, u32[]{:S(2)}) copy-start(bf16[4,1,256,256]{3,2,1,0:T(8,128)(2,1)} %param.23) | copy-start | bytes 1572868
  62.8 63.1 %all-gather.15.cloned.1.call-start = ((), (), s32[]{:S(2)}) async-start(), calls=%async_computation.13 | async-start | bytes 1179648 | tf_op jit(solution)/shard_map/all_gather | solution.py:8
  86.2 71.8 %reduce-scatter.9.cloned.1.call-start = ((), (), s32[]{:S(2)}) async-start(), calls=%async_computation.7 | async-start | bytes 655360 | tf_op jit(solution)/shard_map/reduce_scatter | solution.py:20
  136.4 60.8 %all-gather.17.cloned.1.call-start = ((), (), s32[]{:S(2)}) async-start(), calls=%async_computation.14 | async-start | bytes 1179648 | tf_op jit(solution)/shard_map/all_gather | solution.py:8
  160.0 73.1 %reduce-scatter.11.cloned.1.call-start = ((), (), s32[]{:S(2)}) async-start(), calls=%async_computation.8 | async-start | bytes 655360 | tf_op jit(solution)/shard_map/reduce_scatter | solution.py:20
  206.1 27.0 %copy-start.6 = (bf16[4,1,256,256]{3,2,1,0:T(8,128)(2,1)S(1)}, bf16[4,1,256,256]{3,2,1,0:T(8,128)(2,1)}, u32[]{:S(2)}) copy-start(bf16[4,1,256,256]{3,2,1,0:T(8,128)(2,1)} %param.31) | copy-start | bytes 1572868
  209.1 26.3 %copy-start.9 = (s32[1,1,3,6]{3,1,2,0:T(1,128)S(1)}, s32[1,1,3,6]{3,1,2,0:T(1,128)}, u32[]{:S(2)}) copy-start(s32[1,1,3,6]{3,1,2,0:T(1,128)} %param.29) | copy-start | bytes 220
  209.1 26.4 %copy-start.8 = (s32[1,1,3,6]{3,1,2,0:T(1,128)S(1)}, s32[1,1,3,6]{3,1,2,0:T(1,128)}, u32[]{:S(2)}) copy-start(s32[1,1,3,6]{3,1,2,0:T(1,128)} %param.30) | copy-start | bytes 220
  210.0 62.5 %all-gather.19.cloned.1.call-start = ((), (), s32[]{:S(2)}) async-start(), calls=%async_computation.15 | async-start | bytes 1179648 | tf_op jit(solution)/shard_map/all_gather | solution.py:8
  235.2 73.0 %reduce-scatter.13.cloned.1.call-start = ((), (), s32[]{:S(2)}) async-start(), calls=%async_computation.9 | async-start | bytes 655360 | tf_op jit(solution)/shard_map/reduce_scatter | solution.py:20
  281.7 2.0 copy-start
  283.7 24.5 %copy-start.4 = (f32[256,256]{1,0:T(8,128)S(1)}, f32[256,256]{1,0:T(8,128)}, u32[]{:S(2)}) copy-start(f32[256,256]{1,0:T(8,128)} %get-tuple-element.109) | copy-start | bytes 786436
  285.1 62.3 %all-gather.21.cloned.1.call-start = ((), (), s32[]{:S(2)}) async-start(), calls=%async_computation.16 | async-start | bytes 1179648 | tf_op jit(solution)/shard_map/all_gather | solution.py:8
  310.0 72.5 %reduce-scatter.15.cloned.1.call-start = ((), (), s32[]{:S(2)}) async-start(), calls=%async_computation.10 | async-start | bytes 655360 | tf_op jit(solution)/shard_map/reduce_scatter | solution.py:20
  354.4 1.6 slice-start
  357.2 1.4 copy-start.2
  359.4 62.5 %all-gather.23.cloned.1.call-start = ((), (), s32[]{:S(2)}) async-start(), calls=%async_computation.17 | async-start | bytes 1179648 | tf_op jit(solution)/shard_map/all_gather | solution.py:8
  384.4 70.2 %reduce-scatter.17.cloned.1.call-start = ((), (), s32[]{:S(2)}) async-start(), calls=%async_computation.11 | async-start | bytes 655360 | tf_op jit(solution)/shard_map/reduce_scatter | solution.py:20
  428.9 1.6 copy-start.3
  430.5 24.1 %copy-start.5 = (f32[256,256]{1,0:T(8,128)S(1)}, f32[256,256]{1,0:T(8,128)}, u32[]{:S(2)}) copy-start(f32[256,256]{1,0:T(8,128)} %get-tuple-element.105) | copy-start | bytes 786436
Sparse Core Ops, SparseCore 0:
  9.5 41.2 all-gather.12
  62.9 21.4 reduce-scatter.6
  86.7 39.1 all-gather.14
  136.6 21.4 reduce-scatter.8
  160.1 37.0 all-gather.16
  210.1 22.9 reduce-scatter.10
  235.4 37.1 all-gather.18
  285.2 22.9 reduce-scatter.12
  310.2 37.0 all-gather.20
  359.5 22.9 reduce-scatter.14
  384.8 37.1 all-gather.22
  431.6 22.9 reduce-scatter.16
where the time goes:
time: 466 us; the launch traced here: 464 us
  waiting for transfers between devices  365 us (78%)
  matrix products  41.8 us (9%)
  local copies, waits for them, and re-layouts  39.6 us (8%)
  between operations  13.9 us (3%)
    all_gather x6, waiting for transfers between devices, fetch_sources(): gathered = lax.all_gather(solved_panel, 'row', axis=0, tiled=True)  229 us
    reduce_scatter x6, waiting for transfers between devices, row_share(): lax.psum_scatter(partial_level.astype(jnp.bfloat16), 'col', scatter_dimen...  135 us
    dot_general x6, matrix products, block_updates(): jnp.einsum('kij,kjm->kim', blocks, chosen, preferred_element_type=jnp.flo...  15.9 us
    dot_general x6, matrix products, block_updates(): jnp.einsum('qk,kim->qim', selector, products, precision=lax.Precision.HIG...  13.4 us
    dot_general x6, local copies, waits for them, and re-layouts, block_updates(): jnp.einsum('kij,kjm->kim', blocks, chosen, preferred_element_type=jnp.flo...  13.2 us
    dot_general x7, matrix products, diag_apply(): jnp.einsum('sij,sjm->sim', inverse, vector.astype(jnp.bfloat16), preferre...  12.5 us
  transfers between devices with their start and end apart: 12, of which 12 were waited for; matrix products, arithmetic and copies ran while one was open for 0% of the time, Pallas kernels for 0%

commit v1 on v0

v1 whole, which is shorter than its diff:
```python
import functools

import jax
import jax.numpy as jnp
from jax import lax
from jax.experimental import pallas as pl
from jax.experimental.pallas import tpu as pltpu
from jax.sharding import PartitionSpec as P

MESH = pl.DeviceIdType.MESH
CHUNKS = 2
F32 = jnp.float32
BF16 = jnp.bfloat16


def kernel(
    rows,
    cols,
    levels,
    slots,
    width,
    lanes,
    rhs_ref,
    lower_ref,
    lower_source,
    lower_target,
    diag_lower,
    upper_ref,
    upper_source,
    upper_target,
    diag_upper,
    out_ref,
    *scratch,
):
    rounds = 2 * (levels - 1)
    panels = scratch[: rounds * CHUNKS]
    forward, far, products, owned, outbox, inbox, gather_send, gather_recv, sum_send, sum_recv = scratch[
        rounds * CHUNKS :
    ]
    major = 4 if rows % 4 == 0 else 1
    minor = rows // major
    row, col = lax.axis_index("row"), lax.axis_index("col")
    row_major, row_minor = row // minor, row % minor

    def row_at(major_step, minor_step):
        return ((row_major + major_step) % major) * minor + (row_minor + minor_step) % minor

    peers = [(row_at(step, 0), col) for step in range(1, major)]
    peers += [(row_at(0, step), col) for step in range(1, minor)]
    peers += [(row, (col + step) % cols) for step in range(1, cols)]
    barrier = pltpu.get_barrier_semaphore()
    for peer in peers:
        pl.semaphore_signal(barrier, inc=1, device_id=peer, device_id_type=MESH)

    def lanes_of(chunk):
        return slice(chunk * lanes, (chunk + 1) * lanes)

    def plan(step):
        if step < levels - 1:
            return step, step + 1, lower_ref, lower_source, lower_target, step == 0, list(range(step + 2, levels))
        source = 2 * (levels - 1) - step
        first = step == levels - 1
        return source - 1, source - 1, upper_ref, upper_source, upper_target, first, list(range(source - 1))

    def far_slot(step, level):
        return level - 2 if step < levels - 1 else level

    pending = {}

    def push(step, chunk, slot, target, index):
        ref = panels[step * CHUNKS + chunk]
        copy = pltpu.make_async_remote_copy(
            src_ref=ref.at[slot],
            dst_ref=ref.at[slot],
            send_sem=gather_send.at[chunk, index],
            recv_sem=gather_recv.at[step, chunk, slot],
            device_id=(target, col),
            device_id_type=MESH,
        )
        copy.start()
        pending.setdefault(("gather", step, chunk), []).append(copy)

    def arrived(step, chunk, slot):
        ref = panels[step * CHUNKS + chunk]
        pltpu.make_async_remote_copy(
            src_ref=ref.at[slot],
            dst_ref=ref.at[slot],
            send_sem=gather_send.at[chunk, 0],
            recv_sem=gather_recv.at[step, chunk, slot],
            device_id=(row, col),
            device_id_type=MESH,
        ).wait_recv()

    def drain(kind, step, chunk):
        for copy in pending.pop((kind, step, chunk), []):
            copy.wait_send()

    def gather_start(step, chunk):
        for offset in range(1, minor):
            push(step, chunk, row, row_at(0, offset), offset - 1)
        for offset in range(1, major):
            push(step, chunk, row, row_at(offset, 0), minor - 1 + offset - 1)

    def gather_forward(step, chunk, offset):
        slot = row_at(offset, 0)
        arrived(step, chunk, slot)
        base = (minor - 1) + (major - 1) + (offset - 1) * (minor - 1)
        for across in range(1, minor):
            push(step, chunk, slot, row_at(0, across), base + across - 1)

    def gather_finish(step, chunk):
        for across in range(1, minor):
            for offset in range(major):
                arrived(step, chunk, row_at(offset, across))

    def picked(target_ref, at, wanted):
        total = jnp.zeros((width, lanes), F32)
        for k in range(slots):
            mask = jnp.full((width, lanes), target_ref[0, 0, at, k], jnp.int32) == wanted
            total = total + jnp.where(mask, products[k], 0.0)
        return total

    def update_near(step, chunk):
        at, level, blocks, source, target, first, _ = plan(step)
        ref = panels[step * CHUNKS + chunk]
        for k in range(slots):
            products[k] = jnp.dot(blocks[0, 0, at, k], ref[source[0, 0, at, k]], preferred_element_type=F32)
        drain("sum", step - 1, chunk)
        for offset in list(range(1, cols)) + [0]:
            owner = (col + offset) % cols
            total = picked(target, at, level * cols + owner)
            if not first:
                total = total + far[far_slot(step, level), owner, chunk]
            if offset == 0:
                owned[chunk] = total.astype(BF16)
                continue
            outbox[step, chunk, offset - 1] = total.astype(BF16)
            copy = pltpu.make_async_remote_copy(
                src_ref=outbox.at[step, chunk, offset - 1],
                dst_ref=inbox.at[step, chunk, offset - 1],
                send_sem=sum_send.at[chunk, offset - 1],
                recv_sem=sum_recv.at[step, chunk, offset - 1],
                device_id=(row, owner),
                device_id_type=MESH,
            )
            copy.start()
            pending.setdefault(("sum", step, chunk), []).append(copy)

    def update_far(step, chunk):
        at, _, _, _, target, first, others = plan(step)
        for level in others:
            place = far_slot(step, level)

            @pl.loop(0, cols)
            def _(q):
                total = picked(target, at, level * cols + q)
                if not first:
                    total = total + far[place, q, chunk]
                far[place, q, chunk] = total

    def finish_sum(step, chunk):
        level = plan(step)[1]
        total = owned[chunk].astype(F32)
        for copy in pending[("sum", step, chunk)]:
            copy.wait_recv()
        for offset in range(1, cols):
            total = total + inbox[step, chunk, offset - 1].astype(F32)
        if step < levels - 1:
            solve_lower(level, chunk, rhs_ref[level, 0, :, lanes_of(chunk)].astype(F32) - total)
        else:
            solve_upper(level, chunk, forward[level, chunk] - total)

    def publish(step, chunk, result):
        if step < rounds:
            panels[step * CHUNKS + chunk][row] = result.astype(BF16)
            drain("gather", step - 1, chunk)

    def solve_lower(level, chunk, lowered):
        result = jnp.dot(diag_lower[level, 0], lowered.astype(BF16), preferred_element_type=F32)
        forward[level, chunk] = result
        if level == levels - 1:
            solve_upper(level, chunk, result)
        else:
            publish(level, chunk, result)

    def solve_upper(level, chunk, raised):
        result = jnp.dot(diag_upper[level, 0], raised.astype(BF16), preferred_element_type=F32)
        out_ref[level, 0, :, lanes_of(chunk)] = result
        publish(2 * (levels - 1) - level, chunk, result)

    for chunk in range(CHUNKS):
        solve_lower(0, chunk, rhs_ref[0, 0, :, lanes_of(chunk)].astype(F32))
    pl.semaphore_wait(barrier, len(peers))

    def turn(step, chunk, other_step):
        moving = other_step is not None and other_step < rounds
        other = 1 - chunk
        gather_finish(step, chunk)
        update_near(step, chunk)
        if moving and major > 1:
            gather_forward(other_step, other, 1)
        update_far(step, chunk)
        if moving:
            for offset in range(2, major - 1):
                gather_forward(other_step, other, offset)
        finish_sum(step, chunk)
        if step + 1 < rounds:
            gather_start(step + 1, chunk)
        if moving and major > 2:
            gather_forward(other_step, other, major - 1)

    gather_start(0, 0)
    gather_start(0, 1)
    for offset in range(1, major):
        gather_forward(0, 0, offset)
    for step in range(rounds):
        turn(step, 0, step)
        turn(step, 1, step + 1)
    for kind in ("gather", "sum"):
        for chunk in range(CHUNKS):
            drain(kind, rounds - 1, chunk)


def shards(*args):
    rows, cols = lax.axis_size("row"), lax.axis_size("col")
    levels, per_device, width, rhs_cols = args[0].shape
    slots = args[1].shape[3]
    assert per_device == 1 and rhs_cols % CHUNKS == 0 and levels > 2
    lanes = rhs_cols // CHUNKS
    rounds = 2 * (levels - 1)
    major = 4 if rows % 4 == 0 else 1
    minor = rows // major
    copies = (minor - 1) + (major - 1) + (major - 1) * (minor - 1)
    vmem = pl.BlockSpec(memory_space=pltpu.VMEM)
    smem = pl.BlockSpec(memory_space=pltpu.SMEM)
    scratch = [pltpu.VMEM((rows, width, lanes), BF16) for _ in range(rounds * CHUNKS)]
    scratch += [
        pltpu.VMEM((levels, CHUNKS, width, lanes), F32),
        pltpu.VMEM((levels - 2, cols, CHUNKS, width, lanes), F32),
        pltpu.VMEM((slots, width, lanes), F32),
        pltpu.VMEM((CHUNKS, width, lanes), BF16),
        pltpu.VMEM((rounds, CHUNKS, cols - 1, width, lanes), BF16),
        pltpu.VMEM((rounds, CHUNKS, cols - 1, width, lanes), BF16),
        pltpu.SemaphoreType.DMA((CHUNKS, copies)),
        pltpu.SemaphoreType.DMA((rounds, CHUNKS, rows)),
        pltpu.SemaphoreType.DMA((CHUNKS, cols - 1)),
        pltpu.SemaphoreType.DMA((rounds, CHUNKS, cols - 1)),
    ]
    return pl.pallas_call(
        functools.partial(kernel, rows, cols, levels, slots, width, lanes),
        out_shape=jax.ShapeDtypeStruct(args[0].shape, F32),
        in_specs=[vmem, vmem, smem, smem, vmem, vmem, smem, smem, vmem],
        out_specs=vmem,
        scratch_shapes=scratch,
        compiler_params=pltpu.CompilerParams(
            collective_id=0, has_side_effects=True, vmem_limit_bytes=60 * 1024 * 1024
        ),
    )(*args)


def solution(mesh):
    in_specs = (
        P(None, ("row", "col"), None, None),
        P("row", "col", None, None, None, None),
        P("row", "col", None, None),
        P("row", "col", None, None),
        P(None, ("row", "col"), None, None),
        P("row", "col", None, None, None, None),
        P("row", "col", None, None),
        P("row", "col", None, None),
        P(None, ("row", "col"), None, None),
    )
    out_specs = P(None, ("row", "col"), None, None)
    return jax.shard_map(shards, mesh=mesh, in_specs=in_specs, out_specs=out_specs, check_vma=False)
```

time: 466 us -> 142 us (0.30)
  waiting for transfers between devices: 365 us -> 0 us
  Pallas kernels: 0 us -> 135 us
  matrix products: 41.8 us -> 0 us
  local copies, waits for them, and re-layouts: 39.6 us -> 7.32 us
  between operations: 13.9 us -> 0.01 us
    all_gather x6 -> x0, waiting for transfers between devices: 229 us -> none  [fetch_sources(): gathered = lax.all_gather(solved_panel, 'row', axis=0, tiled=True)]
    reduce_scatter x6 -> x0, waiting for transfers between devices: 135 us -> none  [row_share(): lax.psum_scatter(partial_level.astype(jnp.bfloat16), 'col', scatter_dimen...]
    pallas_call x0 -> x1, Pallas kernels: none -> 135 us  [shards(): pl.pallas_call(functools.partial(kernel, rows, cols, levels, slots, width...]
    dot_general x19 -> x0, matrix products: 41.8 us -> none  [the longest x6 15.9 us: block_updates(): jnp.einsum('kij,kjm->kim', blocks, chosen, preferred_element_type=jnp.flo...]
    dot_general x6 -> x0, local copies, waits for them, and re-layouts: 13.2 us -> none  [block_updates(): jnp.einsum('kij,kjm->kim', blocks, chosen, preferred_element_type=jnp.flo...]
    gather x6 -> x0, local copies, waits for them, and re-layouts: 6.93 us -> none  [fetch_sources(): return jnp.take(gathered, source_ids, axis=0)]
    all_gather x4 -> x0, local copies, waits for them, and re-layouts: 5.9 us -> none  [fetch_sources(): gathered = lax.all_gather(solved_panel, 'row', axis=0, tiled=True)]
  transfers between devices with their start and end apart: 12 -> 0, of which waited for: 12 -> 0; matrix products, arithmetic and copies ran while one was open for 0% -> 0% of each run, Pallas kernels for 0% -> 0%
where the time goes in v1:
time: 142 us
  Pallas kernels  135 us (95%)
  local copies, waits for them, and re-layouts  7.32 us (5%)
    pallas_call x1, Pallas kernels, shards(): pl.pallas_call(functools.partial(kernel, rows, cols, levels, slots, width...  135 us
    unnamed x5, local copies, waits for them, and re-layouts  7.32 us

profile of v1, /device:TPU:1, one launch (start us, length us, event | category | flops | bytes accessed | tf_op | source)
XLA Modules:
  0.0 142.0 jit_solution(4871715295651432958)
XLA Ops:
  0.0 1.3 copy.10.lower_source
  1.3 1.3 copy.11.lower_target
  2.5 1.3 copy.12.upper_source
  3.8 1.2 copy.13.upper_target
  5.0 134.7 %shard_map.91 = f32[4,1,256,256]{3,2,1,0:T(8,128)} custom-call(bf16[4,1,256,256]{3,2,1,0:T(8,128)(2,1)} %rhs_ref.1, bf16[1,1,3,6,256,256]{5,4,3,2,1,0:T(8,128)(2,1)} %lower_ref.1, s32[1,1,3,6]{3,2,1,0:T(4,128)} %copy.10.lower_source, s32[1,1,3,6]{3,2,1,0:T(4,128)} %copy.11.lower_target, bf16[4,1,256,256]{3,2,1,0:T(8,128)(2,1)} %diag_lower.1, ...), custom_call_target="tpu_custom_call" | custom-call | tf_op jit(solution)/shard_map/pallas_call | solution.py:249
  139.7 2.3 %copy.15 = f32[4,1,256,256]{3,2,1,0:T(8,128)} copy(f32[4,1,256,256]{3,2,1,0:T(8,128)} %shard_map.91) | data formatting | bytes 2097152

commit v2 on v1

--- a/solution.py
+++ b/solution.py
@@ -20,23 +20,43 @@
     slots,
     width,
     lanes,
-    rhs_ref,
-    lower_ref,
+    rhs_hbm,
+    lower_hbm,
     lower_source,
     lower_target,
-    diag_lower,
-    upper_ref,
+    diag_lower_hbm,
+    upper_hbm,
     upper_source,
     upper_target,
-    diag_upper,
-    out_ref,
+    diag_upper_hbm,
+    out_hbm,
     *scratch,
 ):
     rounds = 2 * (levels - 1)
     panels = scratch[: rounds * CHUNKS]
-    forward, far, products, owned, outbox, inbox, gather_send, gather_recv, sum_send, sum_recv = scratch[
-        rounds * CHUNKS :
-    ]
+    rest = scratch[rounds * CHUNKS :]
+    forward, far, products, owned, outbox, inbox, gather_send, gather_recv, sum_send, sum_recv = rest[:10]
+    inputs, out_ref, load_sem, store_sem = rest[10:15], rest[15], rest[16], rest[17]
+    sources = (rhs_hbm, diag_lower_hbm, lower_hbm.at[0, 0], diag_upper_hbm, upper_hbm.at[0, 0])
+    order = [(0, 0), (1, 0), (2, 0)]
+    for level in range(1, levels):
+        order += [(0, level), (1, level)] + ([(2, level)] if level < levels - 1 else [])
+    for level in range(levels - 1, -1, -1):
+        order += [(3, level)] + ([(4, level - 1)] if level else [])
+    loaded = set()
+
+    def fetch(ref, index):
+        return pltpu.make_async_copy(sources[ref].at[index], inputs[ref].at[index], load_sem.at[ref, index])
+
+    def load(ref, index):
+        if (ref, index) not in loaded:
+            loaded.add((ref, index))
+            fetch(ref, index).wait()
+        return inputs[ref].at[index]
+
+    def store(level):
+        return pltpu.make_async_copy(out_ref.at[level], out_hbm.at[level], store_sem.at[level])
+
     major = 4 if rows % 4 == 0 else 1
     minor = rows // major
     row, col = lax.axis_index("row"), lax.axis_index("col")
@@ -57,28 +77,37 @@
 
     def plan(step):
         if step < levels - 1:
-            return step, step + 1, lower_ref, lower_source, lower_target, step == 0, list(range(step + 2, levels))
+            return step, step + 1, 2, lower_source, lower_target, step == 0, list(range(step + 2, levels))
         source = 2 * (levels - 1) - step
         first = step == levels - 1
-        return source - 1, source - 1, upper_ref, upper_source, upper_target, first, list(range(source - 1))
+        return source - 1, source - 1, 4, upper_source, upper_target, first, list(range(source - 1))
 
     def far_slot(step, level):
         return level - 2 if step < levels - 1 else level
 
     pending = {}
 
-    def push(step, chunk, slot, target, index):
+    def push(step, chunk, slot, target, index, needed=None):
         ref = panels[step * CHUNKS + chunk]
-        copy = pltpu.make_async_remote_copy(
-            src_ref=ref.at[slot],
-            dst_ref=ref.at[slot],
-            send_sem=gather_send.at[chunk, index],
-            recv_sem=gather_recv.at[step, chunk, slot],
-            device_id=(target, col),
-            device_id_type=MESH,
-        )
-        copy.start()
-        pending.setdefault(("gather", step, chunk), []).append(copy)
+
+        def make():
+            return pltpu.make_async_remote_copy(
+                src_ref=ref.at[slot],
+                dst_ref=ref.at[slot],
+                send_sem=gather_send.at[chunk, index],
+                recv_sem=gather_recv.at[step, chunk, slot],
+                device_id=(target, col),
+                device_id_type=MESH,
+            )
+
+        pending.setdefault(("gather", step, chunk), []).append((make, needed))
+        when(needed, lambda: make().start())
+
+    def when(needed, action):
+        if needed is None:
+            action()
+        else:
+            pl.when(needed)(action)
 
     def arrived(step, chunk, slot):
         ref = panels[step * CHUNKS + chunk]
@@ -92,21 +121,31 @@
         ).wait_recv()
 
     def drain(kind, step, chunk):
-        for copy in pending.pop((kind, step, chunk), []):
-            copy.wait_send()
-
-    def gather_start(step, chunk):
-        for offset in range(1, minor):
-            push(step, chunk, row, row_at(0, offset), offset - 1)
-        for offset in range(1, major):
-            push(step, chunk, row, row_at(offset, 0), minor - 1 + offset - 1)
-
-    def gather_forward(step, chunk, offset):
-        slot = row_at(offset, 0)
-        arrived(step, chunk, slot)
-        base = (minor - 1) + (major - 1) + (offset - 1) * (minor - 1)
+        for make, needed in pending.pop((kind, step, chunk), []):
+            when(needed, lambda: make().wait_send())
+
+    def gather_major(step, chunk):
+        push(step, chunk, row, row + minor, 0, row_major + 1 < major)
+        push(step, chunk, row, row - minor, 1, row_major >= 1)
+
+    def gather_minor(step, chunk):
         for across in range(1, minor):
-            push(step, chunk, slot, row_at(0, across), base + across - 1)
+            push(step, chunk, row, row_at(0, across), 1 + across)
+
+    def relay(step, chunk, hops):
+        if hops >= major:
+            return
+        for side, sign in enumerate((-1, 1)):
+            origin = row_major + sign * hops
+            slot = row + sign * hops * minor
+            came = (origin >= 0) & (origin < major)
+            base = 1 + minor + ((hops - 1) * 2 + side) * minor
+            when(came, lambda: arrived(step, chunk, slot))
+            if hops + 1 < major:
+                after = row_major - sign
+                push(step, chunk, slot, row - sign * minor, base, came & (after >= 0) & (after < major))
+            for across in range(1, minor):
+                push(step, chunk, slot, row_at(0, across), base + across, came)
 
     def gather_finish(step, chunk):
         for across in range(1, minor):
@@ -116,15 +155,16 @@
     def picked(target_ref, at, wanted):
         total = jnp.zeros((width, lanes), F32)
         for k in range(slots):
-            mask = jnp.full((width, lanes), target_ref[0, 0, at, k], jnp.int32) == wanted
+            mask = jnp.full((width, lanes), target_ref[at, 0, k], jnp.int32) == wanted
             total = total + jnp.where(mask, products[k], 0.0)
         return total
 
     def update_near(step, chunk):
         at, level, blocks, source, target, first, _ = plan(step)
         ref = panels[step * CHUNKS + chunk]
+        held = load(blocks, at)
         for k in range(slots):
-            products[k] = jnp.dot(blocks[0, 0, at, k], ref[source[0, 0, at, k]], preferred_element_type=F32)
+            products[k] = jnp.dot(held[k], ref[source[at, 0, k]], preferred_element_type=F32)
         drain("sum", step - 1, chunk)
         for offset in list(range(1, cols)) + [0]:
             owner = (col + offset) % cols
@@ -144,7 +184,7 @@
                 device_id_type=MESH,
             )
             copy.start()
-            pending.setdefault(("sum", step, chunk), []).append(copy)
+            pending.setdefault(("sum", step, chunk), []).append((lambda copy=copy: copy, None))
 
     def update_far(step, chunk):
         at, _, _, _, target, first, others = plan(step)
@@ -161,12 +201,12 @@
     def finish_sum(step, chunk):
         level = plan(step)[1]
         total = owned[chunk].astype(F32)
-        for copy in pending[("sum", step, chunk)]:
-            copy.wait_recv()
+        for make, _ in pending[("sum", step, chunk)]:
+            make().wait_recv()
         for offset in range(1, cols):
             total = total + inbox[step, chunk, offset - 1].astype(F32)
         if step < levels - 1:
-            solve_lower(level, chunk, rhs_ref[level, 0, :, lanes_of(chunk)].astype(F32) - total)
+            solve_lower(level, chunk, load(0, level)[0, :, lanes_of(chunk)].astype(F32) - total)
         else:
             solve_upper(level, chunk, forward[level, chunk] - total)
 
@@ -176,7 +216,7 @@
             drain("gather", step - 1, chunk)
 
     def solve_lower(level, chunk, lowered):
-        result = jnp.dot(diag_lower[level, 0], lowered.astype(BF16), preferred_element_type=F32)
+        result = jnp.dot(load(1, level)[0], lowered.astype(BF16), preferred_element_type=F32)
         forward[level, chunk] = result
         if level == levels - 1:
             solve_upper(level, chunk, result)
@@ -184,41 +224,52 @@
             publish(level, chunk, result)
 
     def solve_upper(level, chunk, raised):
-        result = jnp.dot(diag_upper[level, 0], raised.astype(BF16), preferred_element_type=F32)
+        result = jnp.dot(load(3, level)[0], raised.astype(BF16), preferred_element_type=F32)
         out_ref[level, 0, :, lanes_of(chunk)] = result
+        if chunk == CHUNKS - 1:
+            store(level).start()
         publish(2 * (levels - 1) - level, chunk, result)
 
+    for ref, index in order:
+        fetch(ref, index).start()
     for chunk in range(CHUNKS):
-        solve_lower(0, chunk, rhs_ref[0, 0, :, lanes_of(chunk)].astype(F32))
+        solve_lower(0, chunk, load(0, 0)[0, :, lanes_of(chunk)].astype(F32))
     pl.semaphore_wait(barrier, len(peers))
 
     def turn(step, chunk, other_step):
-        moving = other_step is not None and other_step < rounds
         other = 1 - chunk
+
+        def relay_other(hops):
+            if other_step < rounds:
+                relay(other_step, other, hops)
+
         gather_finish(step, chunk)
         update_near(step, chunk)
-        if moving and major > 1:
-            gather_forward(other_step, other, 1)
+        relay_other(1)
         update_far(step, chunk)
-        if moving:
-            for offset in range(2, major - 1):
-                gather_forward(other_step, other, offset)
+        for hops in range(2, major - 1):
+            relay_other(hops)
         finish_sum(step, chunk)
         if step + 1 < rounds:
-            gather_start(step + 1, chunk)
-        if moving and major > 2:
-            gather_forward(other_step, other, major - 1)
-
-    gather_start(0, 0)
-    gather_start(0, 1)
-    for offset in range(1, major):
-        gather_forward(0, 0, offset)
+            gather_major(step + 1, chunk)
+        if major > 2:
+            relay_other(major - 1)
+        if step + 1 < rounds:
+            gather_minor(step + 1, chunk)
+
+    for chunk in range(CHUNKS):
+        gather_major(0, chunk)
+        gather_minor(0, chunk)
+    for hops in range(1, major):
+        relay(0, 0, hops)
     for step in range(rounds):
         turn(step, 0, step)
         turn(step, 1, step + 1)
     for kind in ("gather", "sum"):
         for chunk in range(CHUNKS):
             drain(kind, rounds - 1, chunk)
+    for level in range(levels):
+        store(level).wait()
 
 
 def shards(*args):
@@ -230,9 +281,10 @@
     rounds = 2 * (levels - 1)
     major = 4 if rows % 4 == 0 else 1
     minor = rows // major
-    copies = (minor - 1) + (major - 1) + (major - 1) * (minor - 1)
-    vmem = pl.BlockSpec(memory_space=pltpu.VMEM)
+    copies = 1 + minor + 2 * (major - 1) * minor
     smem = pl.BlockSpec(memory_space=pltpu.SMEM)
+    anywhere = pl.BlockSpec(memory_space=pl.ANY)
+    args = [arg.reshape(levels - 1, 1, slots) if arg.dtype == jnp.int32 else arg for arg in args]
     scratch = [pltpu.VMEM((rows, width, lanes), BF16) for _ in range(rounds * CHUNKS)]
     scratch += [
         pltpu.VMEM((levels, CHUNKS, width, lanes), F32),
@@ -246,11 +298,19 @@
         pltpu.SemaphoreType.DMA((CHUNKS, cols - 1)),
         pltpu.SemaphoreType.DMA((rounds, CHUNKS, cols - 1)),
     ]
+    scratch += [pltpu.VMEM(args[i].shape[-4:], BF16) for i in (0, 4)]
+    scratch += [pltpu.VMEM(args[1].shape[-4:], BF16)]
+    scratch += [pltpu.VMEM(args[8].shape, BF16), pltpu.VMEM(args[5].shape[-4:], BF16)]
+    scratch += [
+        pltpu.VMEM(args[0].shape, F32),
+        pltpu.SemaphoreType.DMA((5, levels)),
+        pltpu.SemaphoreType.DMA((levels,)),
+    ]
     return pl.pallas_call(
         functools.partial(kernel, rows, cols, levels, slots, width, lanes),
         out_shape=jax.ShapeDtypeStruct(args[0].shape, F32),
-        in_specs=[vmem, vmem, smem, smem, vmem, vmem, smem, smem, vmem],
-        out_specs=vmem,
+        in_specs=[anywhere, anywhere, smem, smem, anywhere, anywhere, smem, smem, anywhere],
+        out_specs=anywhere,
         scratch_shapes=scratch,
         compiler_params=pltpu.CompilerParams(
             collective_id=0, has_side_effects=True, vmem_limit_bytes=60 * 1024 * 1024

time: 142 us -> 131 us (0.923)
  Pallas kernels: 135 us -> 129 us
  local copies, waits for them, and re-layouts: 7.32 us -> 2.29 us
    pallas_call x1, Pallas kernels: 135 us -> 129 us  [shards(): pl.pallas_call(functools.partial(kernel, rows, cols, levels, slots, width...]
    unnamed x5 -> x1, local copies, waits for them, and re-layouts: 7.32 us -> 2.29 us
where the time goes in v2:
time: 131 us
  Pallas kernels  129 us (98%)
  local copies, waits for them, and re-layouts  2.29 us (2%)
    pallas_call x1, Pallas kernels, shards(): pl.pallas_call(functools.partial(kernel, rows, cols, levels, slots, width...  129 us

profile of v2, /device:TPU:1, one launch (start us, length us, event | category | flops | bytes accessed | tf_op | source)
XLA Modules:
  0.0 131.2 jit_solution(17280031883193184177)
XLA Ops:
  0.0 129.0 %shard_map.91 = f32[4,1,256,256]{3,2,1,0:T(8,128)} custom-call(bf16[4,1,256,256]{3,2,1,0:T(8,128)(2,1)} %rhs_hbm.1, bf16[1,1,3,6,256,256]{5,4,3,2,1,0:T(8,128)(2,1)} %lower_hbm.1, s32[3,1,6]{2,1,0:T(1,128)} %bitcast.4, s32[3,1,6]{2,1,0:T(1,128)} %bitcast.5, bf16[4,1,256,256]{3,2,1,0:T(8,128)(2,1)} %diag_lower_hbm.1, ...), custom_call_target="tpu_custom_call" | custom-call | tf_op jit(solution)/shard_map/pallas_call | solution.py:309
  129.0 2.3 %copy.11 = f32[4,1,256,256]{3,2,1,0:T(8,128)} copy(f32[4,1,256,256]{3,2,1,0:T(8,128)} %shard_map.91) | data formatting | bytes 2097152

commit v3 on v2

--- a/solution.py
+++ b/solution.py
@@ -125,27 +125,23 @@
             when(needed, lambda: make().wait_send())
 
     def gather_major(step, chunk):
-        push(step, chunk, row, row + minor, 0, row_major + 1 < major)
-        push(step, chunk, row, row - minor, 1, row_major >= 1)
+        for hops in range(1, major):
+            push(step, chunk, row, row + hops * minor, 2 * hops - 2, row_major + hops < major)
+            push(step, chunk, row, row - hops * minor, 2 * hops - 1, row_major >= hops)
 
     def gather_minor(step, chunk):
         for across in range(1, minor):
-            push(step, chunk, row, row_at(0, across), 1 + across)
+            push(step, chunk, row, row_at(0, across), 2 * major - 3 + across)
 
     def relay(step, chunk, hops):
-        if hops >= major:
-            return
         for side, sign in enumerate((-1, 1)):
             origin = row_major + sign * hops
             slot = row + sign * hops * minor
             came = (origin >= 0) & (origin < major)
-            base = 1 + minor + ((hops - 1) * 2 + side) * minor
+            base = 2 * major - 3 + minor + (2 * hops - 2 + side) * (minor - 1)
             when(came, lambda: arrived(step, chunk, slot))
-            if hops + 1 < major:
-                after = row_major - sign
-                push(step, chunk, slot, row - sign * minor, base, came & (after >= 0) & (after < major))
             for across in range(1, minor):
-                push(step, chunk, slot, row_at(0, across), base + across, came)
+                push(step, chunk, slot, row_at(0, across), base + across - 1, came)
 
     def gather_finish(step, chunk):
         for across in range(1, minor):
@@ -240,28 +236,28 @@
         other = 1 - chunk
 
         def relay_other(hops):
-            if other_step < rounds:
+            if other_step < rounds and hops < major:
                 relay(other_step, other, hops)
 
         gather_finish(step, chunk)
+        relay_other(1)
         update_near(step, chunk)
-        relay_other(1)
+        relay_other(2)
         update_far(step, chunk)
-        for hops in range(2, major - 1):
+        for hops in range(3, major):
             relay_other(hops)
         finish_sum(step, chunk)
         if step + 1 < rounds:
+            gather_minor(step + 1, chunk)
             gather_major(step + 1, chunk)
-        if major > 2:
-            relay_other(major - 1)
-        if step + 1 < rounds:
-            gather_minor(step + 1, chunk)
-
-    for chunk in range(CHUNKS):
-        gather_major(0, chunk)
-        gather_minor(0, chunk)
+
+    gather_minor(0, 0)
+    gather_major(0, 0)
     for hops in range(1, major):
         relay(0, 0, hops)
+        if hops == 1:
+            gather_minor(0, 1)
+            gather_major(0, 1)
     for step in range(rounds):
         turn(step, 0, step)
         turn(step, 1, step + 1)
@@ -281,7 +277,7 @@
     rounds = 2 * (levels - 1)
     major = 4 if rows % 4 == 0 else 1
     minor = rows // major
-    copies = 1 + minor + 2 * (major - 1) * minor
+    copies = 2 * major - 2 + minor - 1 + 2 * (major - 1) * (minor - 1)
     smem = pl.BlockSpec(memory_space=pltpu.SMEM)
     anywhere = pl.BlockSpec(memory_space=pl.ANY)
     args = [arg.reshape(levels - 1, 1, slots) if arg.dtype == jnp.int32 else arg for arg in args]

time: 131 us -> 137 us (1.046)
  Pallas kernels: 129 us -> 134 us
    pallas_call x1, Pallas kernels: 129 us -> 134 us  [shards(): pl.pallas_call(functools.partial(kernel, rows, cols, levels, slots, width...]
where the time goes in v3:
time: 137 us
  Pallas kernels  134 us (98%)
  local copies, waits for them, and re-layouts  2.29 us (2%)
    pallas_call x1, Pallas kernels, shards(): pl.pallas_call(functools.partial(kernel, rows, cols, levels, slots, width...  134 us

profile of v3, /device:TPU:1, one launch (start us, length us, event | category | flops | bytes accessed | tf_op | source)
XLA Modules:
  0.0 136.5 jit_solution(3936215839480730363)
XLA Ops:
  0.0 134.2 %shard_map.91 = f32[4,1,256,256]{3,2,1,0:T(8,128)} custom-call(bf16[4,1,256,256]{3,2,1,0:T(8,128)(2,1)} %rhs_hbm.1, bf16[1,1,3,6,256,256]{5,4,3,2,1,0:T(8,128)(2,1)} %lower_hbm.1, s32[3,1,6]{2,1,0:T(1,128)} %bitcast.4, s32[3,1,6]{2,1,0:T(1,128)} %bitcast.5, bf16[4,1,256,256]{3,2,1,0:T(8,128)(2,1)} %diag_lower_hbm.1, ...), custom_call_target="tpu_custom_call" | custom-call | tf_op jit(solution)/shard_map/pallas_call | solution.py:305
  134.2 2.3 %copy.11 = f32[4,1,256,256]{3,2,1,0:T(8,128)} copy(f32[4,1,256,256]{3,2,1,0:T(8,128)} %shard_map.91) | data formatting | bytes 2097152

commit v4 on v2

--- a/solution.py
+++ b/solution.py
@@ -35,7 +35,7 @@
     rounds = 2 * (levels - 1)
     panels = scratch[: rounds * CHUNKS]
     rest = scratch[rounds * CHUNKS :]
-    forward, far, products, owned, outbox, inbox, gather_send, gather_recv, sum_send, sum_recv = rest[:10]
+    forward, far, sums, owned, outbox, inbox, gather_send, gather_recv, sum_send, sum_recv = rest[:10]
     inputs, out_ref, load_sem, store_sem = rest[10:15], rest[15], rest[16], rest[17]
     sources = (rhs_hbm, diag_lower_hbm, lower_hbm.at[0, 0], diag_upper_hbm, upper_hbm.at[0, 0])
     order = [(0, 0), (1, 0), (2, 0)]
@@ -152,23 +152,25 @@
             for offset in range(major):
                 arrived(step, chunk, row_at(offset, across))
 
-    def picked(target_ref, at, wanted):
-        total = jnp.zeros((width, lanes), F32)
-        for k in range(slots):
-            mask = jnp.full((width, lanes), target_ref[at, 0, k], jnp.int32) == wanted
-            total = total + jnp.where(mask, products[k], 0.0)
-        return total
+    def last_slot(target, at, wanted, before):
+        found = jnp.int32(slots)
+        for k in range(before):
+            found = jnp.where(target[at, 0, k] == wanted, k, found)
+        return found
 
     def update_near(step, chunk):
         at, level, blocks, source, target, first, _ = plan(step)
         ref = panels[step * CHUNKS + chunk]
         held = load(blocks, at)
         for k in range(slots):
-            products[k] = jnp.dot(held[k], ref[source[at, 0, k]], preferred_element_type=F32)
+            total = jnp.dot(held[k], ref[source[at, 0, k]], preferred_element_type=F32)
+            if k > 0:
+                total = total + sums[last_slot(target, at, target[at, 0, k], k)]
+            sums[k] = total
         drain("sum", step - 1, chunk)
         for offset in list(range(1, cols)) + [0]:
             owner = (col + offset) % cols
-            total = picked(target, at, level * cols + owner)
+            total = sums[last_slot(target, at, level * cols + owner, slots)]
             if not first:
                 total = total + far[far_slot(step, level), owner, chunk]
             if offset == 0:
@@ -193,7 +195,7 @@
 
             @pl.loop(0, cols)
             def _(q):
-                total = picked(target, at, level * cols + q)
+                total = sums[last_slot(target, at, level * cols + q, slots)]
                 if not first:
                     total = total + far[place, q, chunk]
                 far[place, q, chunk] = total
@@ -232,6 +234,7 @@
 
     for ref, index in order:
         fetch(ref, index).start()
+    sums[slots] = jnp.zeros((width, lanes), F32)
     for chunk in range(CHUNKS):
         solve_lower(0, chunk, load(0, 0)[0, :, lanes_of(chunk)].astype(F32))
     pl.semaphore_wait(barrier, len(peers))
@@ -240,28 +243,28 @@
         other = 1 - chunk
 
         def relay_other(hops):
-            if other_step < rounds:
+            if other_step < rounds and hops < major:
                 relay(other_step, other, hops)
 
         gather_finish(step, chunk)
+        relay_other(1)
         update_near(step, chunk)
-        relay_other(1)
+        relay_other(2)
         update_far(step, chunk)
-        for hops in range(2, major - 1):
+        for hops in range(3, major):
             relay_other(hops)
         finish_sum(step, chunk)
         if step + 1 < rounds:
             gather_major(step + 1, chunk)
-        if major > 2:
-            relay_other(major - 1)
-        if step + 1 < rounds:
             gather_minor(step + 1, chunk)
 
-    for chunk in range(CHUNKS):
-        gather_major(0, chunk)
-        gather_minor(0, chunk)
+    gather_major(0, 0)
+    gather_minor(0, 0)
     for hops in range(1, major):
         relay(0, 0, hops)
+        if hops == 1:
+            gather_major(0, 1)
+            gather_minor(0, 1)
     for step in range(rounds):
         turn(step, 0, step)
         turn(step, 1, step + 1)
@@ -289,7 +292,7 @@
     scratch += [
         pltpu.VMEM((levels, CHUNKS, width, lanes), F32),
         pltpu.VMEM((levels - 2, cols, CHUNKS, width, lanes), F32),
-        pltpu.VMEM((slots, width, lanes), F32),
+        pltpu.VMEM((slots + 1, width, lanes), F32),
         pltpu.VMEM((CHUNKS, width, lanes), BF16),
         pltpu.VMEM((rounds, CHUNKS, cols - 1, width, lanes), BF16),
         pltpu.VMEM((rounds, CHUNKS, cols - 1, width, lanes), BF16),

time: 131 us -> 137 us (1.046)
  Pallas kernels: 129 us -> 135 us
    pallas_call x1, Pallas kernels: 129 us -> 135 us  [shards(): pl.pallas_call(functools.partial(kernel, rows, cols, levels, slots, width...]
where the time goes in v4:
time: 137 us
  Pallas kernels  135 us (99%)
  local copies, waits for them, and re-layouts  2.29 us (2%)
    pallas_call x1, Pallas kernels, shards(): pl.pallas_call(functools.partial(kernel, rows, cols, levels, slots, width...  135 us

profile of v4, /device:TPU:1, one launch (start us, length us, event | category | flops | bytes accessed | tf_op | source)
XLA Modules:
  0.0 136.8 jit_solution(5248876554670353938)
XLA Ops:
  0.0 134.5 %shard_map.91 = f32[4,1,256,256]{3,2,1,0:T(8,128)} custom-call(bf16[4,1,256,256]{3,2,1,0:T(8,128)(2,1)} %rhs_hbm.1, bf16[1,1,3,6,256,256]{5,4,3,2,1,0:T(8,128)(2,1)} %lower_hbm.1, s32[3,1,6]{2,1,0:T(1,128)} %bitcast.4, s32[3,1,6]{2,1,0:T(1,128)} %bitcast.5, bf16[4,1,256,256]{3,2,1,0:T(8,128)(2,1)} %diag_lower_hbm.1, ...), custom_call_target="tpu_custom_call" | custom-call | tf_op jit(solution)/shard_map/pallas_call | solution.py:312
  134.5 2.3 %copy.11 = f32[4,1,256,256]{3,2,1,0:T(8,128)} copy(f32[4,1,256,256]{3,2,1,0:T(8,128)} %shard_map.91) | data formatting | bytes 2097152

commit v5 on v4

--- a/solution.py
+++ b/solution.py
@@ -124,32 +124,46 @@
         for make, needed in pending.pop((kind, step, chunk), []):
             when(needed, lambda: make().wait_send())
 
+    longest = major - 1
+    at_end = (row_major == 0) | (row_major == longest)
+    opposite = (longest - row_major) * minor + row_minor
+    forwarded = 2 + minor
+
     def gather_major(step, chunk):
-        push(step, chunk, row, row + minor, 0, row_major + 1 < major)
-        push(step, chunk, row, row - minor, 1, row_major >= 1)
+        push(step, chunk, row, row + minor, 0, row_major < longest)
+        push(step, chunk, row, row - minor, 1, row_major > 0)
+        if longest > 1:
+            push(step, chunk, row, opposite, 2, at_end)
 
     def gather_minor(step, chunk):
         for across in range(1, minor):
             push(step, chunk, row, row_at(0, across), 1 + across)
 
+    def cross(step, chunk):
+        for across in range(1, minor):
+            slot = row_at(0, across)
+            arrived(step, chunk, slot)
+            if longest > 1:
+                push(step, chunk, slot, opposite, forwarded + across - 1, at_end)
+
     def relay(step, chunk, hops):
-        if hops >= major:
-            return
         for side, sign in enumerate((-1, 1)):
             origin = row_major + sign * hops
             slot = row + sign * hops * minor
             came = (origin >= 0) & (origin < major)
-            base = 1 + minor + ((hops - 1) * 2 + side) * minor
+            base = forwarded + minor - 1 + ((hops - 1) * 2 + side) * minor
             when(came, lambda: arrived(step, chunk, slot))
-            if hops + 1 < major:
+            if hops + 1 < max(longest, 2):
                 after = row_major - sign
                 push(step, chunk, slot, row - sign * minor, base, came & (after >= 0) & (after < major))
             for across in range(1, minor):
                 push(step, chunk, slot, row_at(0, across), base + across, came)
 
     def gather_finish(step, chunk):
+        if longest > 1:
+            when(at_end, lambda: arrived(step, chunk, opposite))
         for across in range(1, minor):
-            for offset in range(major):
+            for offset in range(1, major):
                 arrived(step, chunk, row_at(offset, across))
 
     def last_slot(target, at, wanted, before):
@@ -242,29 +256,27 @@
     def turn(step, chunk, other_step):
         other = 1 - chunk
 
-        def relay_other(hops):
-            if other_step < rounds and hops < major:
+        moving = other_step < rounds
+        gather_finish(step, chunk)
+        update_near(step, chunk)
+        if moving:
+            cross(other_step, other)
+            relay(other_step, other, 1)
+        update_far(step, chunk)
+        if moving:
+            for hops in range(2, longest):
                 relay(other_step, other, hops)
-
-        gather_finish(step, chunk)
-        relay_other(1)
-        update_near(step, chunk)
-        relay_other(2)
-        update_far(step, chunk)
-        for hops in range(3, major):
-            relay_other(hops)
         finish_sum(step, chunk)
         if step + 1 < rounds:
+            gather_minor(step + 1, chunk)
             gather_major(step + 1, chunk)
-            gather_minor(step + 1, chunk)
-
-    gather_major(0, 0)
-    gather_minor(0, 0)
-    for hops in range(1, major):
+
+    for chunk in range(CHUNKS):
+        gather_minor(0, chunk)
+        gather_major(0, chunk)
+    cross(0, 0)
+    for hops in range(1, longest):
         relay(0, 0, hops)
-        if hops == 1:
-            gather_major(0, 1)
-            gather_minor(0, 1)
     for step in range(rounds):
         turn(step, 0, step)
         turn(step, 1, step + 1)
@@ -279,12 +291,12 @@
     rows, cols = lax.axis_size("row"), lax.axis_size("col")
     levels, per_device, width, rhs_cols = args[0].shape
     slots = args[1].shape[3]
-    assert per_device == 1 and rhs_cols % CHUNKS == 0 and levels > 2
+    assert per_device == 1 and rows % 4 == 0 and rhs_cols % CHUNKS == 0 and levels > 2
     lanes = rhs_cols // CHUNKS
     rounds = 2 * (levels - 1)
     major = 4 if rows % 4 == 0 else 1
     minor = rows // major
-    copies = 1 + minor + 2 * (major - 1) * minor
+    copies = 1 + 2 * minor + 2 * (major - 1) * minor
     smem = pl.BlockSpec(memory_space=pltpu.SMEM)
     anywhere = pl.BlockSpec(memory_space=pl.ANY)
     args = [arg.reshape(levels - 1, 1, slots) if arg.dtype == jnp.int32 else arg for arg in args]

time: 137 us -> 125 us (0.912); the launches traced: 137 us -> 127 us
  Pallas kernels: 135 us -> 124 us
    pallas_call x1, Pallas kernels: 135 us -> 124 us  [shards(): pl.pallas_call(functools.partial(kernel, rows, cols, levels, slots, width...]
where the time goes in v5:
time: 125 us; the launch traced here: 127 us
  Pallas kernels  124 us (99%)
  local copies, waits for them, and re-layouts  2.29 us (2%)
    pallas_call x1, Pallas kernels, shards(): pl.pallas_call(functools.partial(kernel, rows, cols, levels, slots, width...  124 us

profile of v5, /device:TPU:1, one launch (start us, length us, event | category | flops | bytes accessed | tf_op | source)
XLA Modules:
  0.0 126.6 jit_solution(1309165786636720762)
XLA Ops:
  0.0 124.3 %shard_map.91 = f32[4,1,256,256]{3,2,1,0:T(8,128)} custom-call(bf16[4,1,256,256]{3,2,1,0:T(8,128)(2,1)} %rhs_hbm.1, bf16[1,1,3,6,256,256]{5,4,3,2,1,0:T(8,128)(2,1)} %lower_hbm.1, s32[3,1,6]{2,1,0:T(1,128)} %bitcast.4, s32[3,1,6]{2,1,0:T(1,128)} %bitcast.5, bf16[4,1,256,256]{3,2,1,0:T(8,128)(2,1)} %diag_lower_hbm.1, ...), custom_call_target="tpu_custom_call" | custom-call | tf_op jit(solution)/shard_map/pallas_call | solution.py:324
  124.3 2.3 %copy.11 = f32[4,1,256,256]{3,2,1,0:T(8,128)} copy(f32[4,1,256,256]{3,2,1,0:T(8,128)} %shard_map.91) | data formatting | bytes 2097152

commit v6 on v5

--- a/solution.py
+++ b/solution.py
@@ -263,13 +263,13 @@
             cross(other_step, other)
             relay(other_step, other, 1)
         update_far(step, chunk)
-        if moving:
-            for hops in range(2, longest):
-                relay(other_step, other, hops)
         finish_sum(step, chunk)
         if step + 1 < rounds:
             gather_minor(step + 1, chunk)
             gather_major(step + 1, chunk)
+        if moving:
+            for hops in range(2, longest):
+                relay(other_step, other, hops)
 
     for chunk in range(CHUNKS):
         gather_minor(0, chunk)

time: 125 us -> 135 us (1.080); the launches traced: 127 us -> 134 us
  Pallas kernels: 124 us -> 132 us
    pallas_call x1, Pallas kernels: 124 us -> 132 us  [shards(): pl.pallas_call(functools.partial(kernel, rows, cols, levels, slots, width...]
where the time goes in v6:
time: 135 us; the launch traced here: 134 us
  Pallas kernels  132 us (98%)
  local copies, waits for them, and re-layouts  2.29 us (2%)
    pallas_call x1, Pallas kernels, shards(): pl.pallas_call(functools.partial(kernel, rows, cols, levels, slots, width...  132 us

profile of v6, /device:TPU:1, one launch (start us, length us, event | category | flops | bytes accessed | tf_op | source)
XLA Modules:
  0.0 133.8 jit_solution(9609199344206525765)
XLA Ops:
  0.0 131.5 %shard_map.91 = f32[4,1,256,256]{3,2,1,0:T(8,128)} custom-call(bf16[4,1,256,256]{3,2,1,0:T(8,128)(2,1)} %rhs_hbm.1, bf16[1,1,3,6,256,256]{5,4,3,2,1,0:T(8,128)(2,1)} %lower_hbm.1, s32[3,1,6]{2,1,0:T(1,128)} %bitcast.4, s32[3,1,6]{2,1,0:T(1,128)} %bitcast.5, bf16[4,1,256,256]{3,2,1,0:T(8,128)(2,1)} %diag_lower_hbm.1, ...), custom_call_target="tpu_custom_call" | custom-call | tf_op jit(solution)/shard_map/pallas_call | solution.py:324
  131.6 2.3 %copy.11 = f32[4,1,256,256]{3,2,1,0:T(8,128)} copy(f32[4,1,256,256]{3,2,1,0:T(8,128)} %shard_map.91) | data formatting | bytes 2097152
